TPU v7x, 128 devices: a whole 4x4x4 slice. The times are simulated.
128 devices in a mesh: grid: 32 (over y, x, z_hi), layer: 4 (over z_lo, core).
Axes of the slice: x: 4, y: 4, z: 4 (z_hi: 2, z_lo: 2; z = z_hi * 2 + z_lo), core: 2. Of those that a mesh axis runs over, the one named last changes fastest.
Arguments:
- a_blocks: bfloat16 [128, 28, 4096], P('grid', 'layer'), may hold values from -0.125 to 0.125
- a_cols: int32 [128, 28], P('grid', 'layer'), may hold values from 0 to 127, as said below
- p_blocks: bfloat16 [128, 28, 4096], P(('grid', 'layer')), may hold values from -6 to 6
- slots: int32 [128, 28, 28], P('grid', 'layer'), may hold values from 0 to 127, as said below
Outputs:
- c_blocks: bfloat16 [128, 128, 4096], P(('grid', 'layer'))
Inputs may be any that keep to these rules, and one draw needn't show every extreme that they name: `a_cols`: position k of every row names a block row i of p_blocks with (i) modulo the number of devices along layer equal to k // 7. The 28 entries of slots[r, k] are all different; entries for different k of one row may repeat.
All inputs are finite; a program needn't handle non-finite values.
Results may differ from a plain program's by a relative error of at most 0.001.
Values may be sent and summed in bfloat16 or wider, within the bound.
A program may use at most 128 MiB of HBM per device.

v0:
```python
import jax
import jax.numpy as jnp
from jax import lax
from jax.sharding import PartitionSpec as P

BS = 64
PROLONG_BLOCKS = 28
PRODUCT_BLOCKS = 128


def row_products(a_rows, table, index_rows, slot_rows):

    def one_row(items):
        a_row, index_row, slot_row = items
        count = a_row.shape[0]
        left = a_row.reshape(count, BS, BS)
        right = jnp.take(table, index_row, axis=0).reshape(count, PROLONG_BLOCKS, BS, BS)
        flipped = jnp.einsum("kmbc,kab->kmca", right, left, preferred_element_type=jnp.float32)
        summed = jax.ops.segment_sum(
            flipped.reshape(count * PROLONG_BLOCKS, BS * BS),
            slot_row.reshape(-1),
            num_segments=PRODUCT_BLOCKS,
        )
        return (
            summed.reshape(PRODUCT_BLOCKS, BS, BS)
            .transpose(0, 2, 1)
            .reshape(PRODUCT_BLOCKS, BS * BS)
        )

    return lax.map(one_row, (a_rows, index_rows, slot_rows))


def per_device(a_blocks, a_cols, p_blocks, slots):
    rows_a, cols_a, slot_a = (
        lax.all_to_all(a_blocks, "layer", split_axis=0, concat_axis=1, tiled=True),
        lax.all_to_all(a_cols, "layer", split_axis=0, concat_axis=1, tiled=True),
        lax.all_to_all(slots, "layer", split_axis=0, concat_axis=1, tiled=True),
    )
    gathered = lax.all_gather(p_blocks, ("grid", "layer"), axis=0, tiled=True)
    return row_products(rows_a, gathered, cols_a, slot_a).astype(jnp.bfloat16)


def solution(mesh):
    placed = (
        P("grid", "layer", None),
        P("grid", "layer"),
        P(("grid", "layer"), None, None),
        P("grid", "layer", None),
    )
    return jax.shard_map(
        per_device,
        mesh=mesh,
        in_specs=placed,
        out_specs=P(("grid", "layer"), None, None),
        check_vma=False,
    )
```

profile of v0, /device:TPU:1, one launch (start us, length us, event | category | flops | bytes accessed | tf_op | source)
XLA Modules:
  0.0 235.1 jit_solution(269203593723154235)
XLA Ops:
  6.5 0.7 all-gather.2.cloned.1.call-update
  7.3 4.7 %all-to-all-start.1 = ((s32[4,1,7]{2,1,0:T(1,128)}), s32[4,1,7]{2,1,0:T(1,128)S(1)}, u32[]{:S(2)}, u32[]{:S(2)}) async-start(s32[4,1,7]{2,1,0:T(1,128)} %bitcast.18), calls=%async_computation.1 | async-start | bytes 4096 | tf_op jit(solution)/shard_map/all_to_all | solution.py:36
  12.0 0.7 copy.19
  12.7 0.7 reshape.122
  13.3 1.8 copy.22
  15.1 3.7 %all-to-all-start = ((s32[4,1,196]{2,1,0:T(1,128)}), s32[4,1,196]{2,1,0:T(1,128)S(1)}, u32[]{:S(2)}, u32[]{:S(2)}) async-start(s32[4,1,196]{2,1,0:T(1,128)} %reshape.122), calls=%async_computation | async-start | bytes 8192 | tf_op jit(solution)/shard_map/all_to_all | solution.py:37
  18.9 0.6 broadcast.54
  19.5 0.7 reduce.5
  20.3 1.5 all-to-all-done
  21.8 4.1 %all-to-all-start.2 = ((bf16[4,7,4096]{2,1,0:T(8,128)(2,1)}), bf16[4,7,4096]{2,1,0:T(8,128)(2,1)S(1)}, u32[]{:S(2)}, u32[]{:S(2)}) async-start(bf16[4,7,4096]{2,1,0:T(8,128)(2,1)} %copy.22), calls=%async_computation.2 | async-start | bytes 524288 | tf_op jit(solution)/shard_map/all_to_all | solution.py:35
  25.9 0.5 broadcast.55
  26.4 0.6 reduce.6
  27.2 3.9 %all-to-all-done.2 = bf16[4,7,4096]{2,1,0:T(8,128)(2,1)S(1)} async-done(((bf16[4,7,4096]{2,1,0:T(8,128)(2,1)}), bf16[4,7,4096]{2,1,0:T(8,128)(2,1)S(1)}, u32[]{:S(2)}, u32[]{:S(2)}) %all-to-all-start.2) | async-done | bytes 229408 | tf_op jit(solution)/shard_map/all_to_all | solution.py:35
  31.1 0.4 reshape.106
  31.6 89.2 %all-gather.2.cloned.1.call-done = bf16[128,28,4096]{2,1,0:T(8,128)(2,1)} async-done(((bf16[1,28,4096]{2,1,0:T(8,128)(2,1)}), bf16[128,28,4096]{2,1,0:T(8,128)(2,1)}) %all-gather.2.cloned.1.call-update) | async-done | bytes 29360144 | tf_op jit(solution)/shard_map/all_gather | solution.py:39
  120.7 7.2 %gather_fusion = bf16[28,28,4096]{2,1,0:T(8,128)(2,1)} fusion(bf16[128,28,4096]{2,1,0:T(8,128)(2,1)} %all-gather.2.cloned.1.call-done, s32[1024]{0:T(1024)S(1)} %pad_clamp_fusion), kind=kCustom, calls=%fused_computation | custom fusion | bytes 12845168 | tf_op jit(solution)/shard_map/while/body/eval_jaxpr/jit(_take)/gather | solution.py:17
  127.9 17.6 %gather.8 = bf16[28,28,64,64]{3,2,1,0:T(8,128)(2,1)} reshape(bf16[28,28,4096]{2,1,0:T(8,128)(2,1)} %gather_fusion) | data formatting | bytes 12845056 | tf_op jit(solution)/shard_map/while/body/eval_jaxpr/jit(_take)/gather | solution.py:17
  145.5 17.8 %copy.21 = bf16[28,28,64,64]{2,3,1,0:T(8,128)(2,1)} copy(bf16[28,28,64,64]{3,2,1,0:T(8,128)(2,1)} %gather.8) | data formatting | bytes 12845056 | tf_op jit(solution)/shard_map/while/body/eval_jaxpr/jit(_take)/gather | solution.py:17
  163.3 13.1 %fusion = f32[28,28,64,64]{3,2,1,0:T(8,128)} fusion(bf16[28,28,64,64]{2,3,1,0:T(8,128)(2,1)} %copy.21, pred[28]{0:T(512)(128)(4,1)S(1)} %compare_and_fusion, bf16[28,64,64,1]{2,1,0,3:T(8,128)(2,1)S(1)} %reshape.106), kind=kOutput, calls=%fused_computation.2 | convolution fusion | flops 414253056 | bytes 19496988 | tf_op jit(solution)/shard_map/while/body/eval_jaxpr/kmbc,kab->kmca/dot_general | solution.py:18
  176.5 21.7 %reshape.101 = f32[784,4096]{1,0:T(8,128)} reshape(f32[28,28,64,64]{3,2,1,0:T(8,128)} %fusion) | data formatting | bytes 25690112 | tf_op jit(solution)/shard_map/while/body/eval_jaxpr/reshape | solution.py:20
  198.1 27.4 %scatter_custom_fusion = f32[128,4096]{1,0:T(8,128)S(1)} fusion(s32[784]{0:T(1024)S(1)} %reshape.99, f32[784,4096]{1,0:T(8,128)} %reshape.101, f32[]{:T(128)} %constant.32.clone.1), kind=kCustom, calls=%fused_computation.6 | custom fusion | flops 3211264 | bytes 2097664 | tf_op jit(solution)/shard_map/while/body/eval_jaxpr/scatter-add | solution.py:19
  225.6 0.7 copy.23
  226.3 0.7 copy.24
  227.0 1.3 copy.25
  (10 shorter events, 0.5 us)
Async XLA Ops:
  6.5 114.2 %all-gather.2.cloned.1.call-start = ((), (), s32[]{:S(2)}) async-start(), calls=%async_computation.3 | async-start | bytes 33816576 | tf_op jit(solution)/shard_map/all_gather | solution.py:39
  7.3 7.9 %all-to-all-start.1 = ((s32[4,1,7]{2,1,0:T(1,128)}), s32[4,1,7]{2,1,0:T(1,128)S(1)}, u32[]{:S(2)}, u32[]{:S(2)}) async-start(s32[4,1,7]{2,1,0:T(1,128)} %bitcast.18), calls=%async_computation.1 | async-start | bytes 4096 | tf_op jit(solution)/shard_map/all_to_all | solution.py:36
  15.1 6.6 %all-to-all-start = ((s32[4,1,196]{2,1,0:T(1,128)}), s32[4,1,196]{2,1,0:T(1,128)S(1)}, u32[]{:S(2)}, u32[]{:S(2)}) async-start(s32[4,1,196]{2,1,0:T(1,128)} %reshape.122), calls=%async_computation | async-start | bytes 8192 | tf_op jit(solution)/shard_map/all_to_all | solution.py:37
  21.8 9.4 %all-to-all-start.2 = ((bf16[4,7,4096]{2,1,0:T(8,128)(2,1)}), bf16[4,7,4096]{2,1,0:T(8,128)(2,1)S(1)}, u32[]{:S(2)}, u32[]{:S(2)}) async-start(bf16[4,7,4096]{2,1,0:T(8,128)(2,1)} %copy.22), calls=%async_computation.2 | async-start | bytes 524288 | tf_op jit(solution)/shard_map/all_to_all | solution.py:35
Sparse Core Ops, SparseCore 0:
  10.3 110.3 all-gather.1
where the time goes:
time: 237 us; the launch traced here: 235 us
  waiting for transfers between devices  95.2 us (40%)
  local copies, waits for them, and re-layouts  72 us (30%)
  other arithmetic  28.8 us (12%)
  between operations  13.4 us (6%)
  matrix products  13.1 us (6%)
  starting transfers between devices  12.5 us (5%)
    all_gather x1, waiting for transfers between devices, per_device(): gathered = lax.all_gather(p_blocks, ('grid', 'layer'), axis=0, tiled=True)  89.2 us
    gather x3, local copies, waits for them, and re-layouts, one_row(): jnp.take(table, index_row, axis=0).reshape(count, PROLONG_BLOCKS, BS, BS)  42.6 us
    scatter-add x1, other arithmetic, one_row(): jax.ops.segment_sum(flipped.reshape(count * PROLONG_BLOCKS, BS * BS), slo...  27.4 us
    reshape x1, local copies, waits for them, and re-layouts, one_row(): flipped.reshape(count * PROLONG_BLOCKS, BS * BS)  21.7 us
    dot_general x1, matrix products, one_row(): jnp.einsum('kmbc,kab->kmca', right, left, preferred_element_type=jnp.floa...  13.1 us
  transfers between devices with their start and end apart: 4, of which 3 were waited for; matrix products, arithmetic and copies ran while one was open for 3% of the time, Pallas kernels for 0%

commit v1 on v0

v1 whole, which is shorter than its diff:
```python
import jax
import jax.numpy as jnp
from jax import lax
from jax.experimental import pallas as pl
from jax.experimental.pallas import tpu as pltpu
from jax.sharding import PartitionSpec as P

MESH = pl.DeviceIdType.MESH
ROWS = 112
ALL, LO, HI = (0, 4), (0, 2), (2, 4)
LANE_OF = {0: 0, -1: 1, 1: 2, 2: 3}


def place():
    g, l = lax.axis_index("grid"), lax.axis_index("layer")
    return g // 8, (g // 2) % 4, (g % 2) * 4 + l


def dev(y, x, j):
    return ((y * 4 + x) * 2 + j // 4, j % 4)


def m4(v):
    return lax.rem(v + 4, 4)


def kernel(
    src, a_src, slot_src, col_src, out,
    pall, abuf, sbuf, cbuf, csm, prod_hi, prod_lo, obuf,
    zs, zr, as_, ar, is_, ir, cs, cr, ls, ss, rs, os, orr, smem_sem,
):
    y, x, j = place()
    q = y * 4 + x
    barrier = pltpu.get_barrier_semaphore()
    peers = [dev(y, x, lax.rem(j + d, 8)) for d in range(1, 8)]
    peers += [
        dev(y, m4(x + 1), j), dev(y, m4(x - 1), j),
        dev(m4(y + 1), x, j), dev(m4(y - 1), x, j),
    ]
    for p in peers:
        pl.semaphore_signal(barrier, inc=1, device_id=p, device_id_type=MESH)
    pl.semaphore_wait(barrier, len(peers))

    def remote(s, d, ssem, rsem, to):
        return pltpu.make_async_remote_copy(
            src_ref=s, dst_ref=d, send_sem=ssem, recv_sem=rsem, device_id=to, device_id_type=MESH
        )

    half, layer = j // 4, j % 4
    own = [
        pltpu.make_async_copy(src.at[j], pall.at[q, j], ls.at[0]),
        pltpu.make_async_copy(a_src, abuf.at[layer, pl.ds(half * 4, 4)], ls.at[1]),
        pltpu.make_async_copy(slot_src, sbuf.at[layer, pl.ds(half * 4, 4)], ls.at[2]),
        pltpu.make_async_copy(col_src, cbuf.at[layer, half], ls.at[3]),
    ]
    for c in own:
        c.start()
    column = []
    for d in range(1, 8):
        t = lax.rem(j + d, 8)
        c = remote(src.at[t], pall.at[q, j], zs.at[d], zr.at[d], dev(y, x, t))
        c.start()
        column.append(c)
    later = []
    for d in range(1, 8):
        to = dev(y, x, lax.rem(j + d, 8))
        later += [
            remote(slot_src, sbuf.at[layer, pl.ds(half * 4, 4)], is_.at[d], ir.at[d], to),
            remote(col_src, cbuf.at[layer, half], cs.at[d], cr.at[d], to),
            remote(a_src, abuf.at[layer, pl.ds(half * 4, 4)], as_.at[d], ar.at[d], to),
        ]
    for c in own:
        c.wait()
    for c in column:
        c.wait_recv()

    sent = []

    def block(h, ident, aoff, boff, rows, axis, step):
        if h == 0:
            bx, by = m4(x + aoff), m4(y + boff)
        else:
            by, bx = m4(y + aoff), m4(x + boff)
        if (axis == "a") == (h == 0):
            to = dev(y, m4(x + step), j)
        else:
            to = dev(m4(y + step), x, j)
        ref = pall.at[by * 4 + bx, pl.ds(4 * h + rows[0], rows[1] - rows[0])]
        return remote(ref, ref, ss.at[h, ident], rs.at[h, ident], to)

    def send(*args):
        c = block(*args)
        c.start()
        sent.append(c)

    def recv(h, ident, aoff, boff, rows):
        block(h, ident, aoff, boff, rows, "a", 1).wait_recv()

    for h in (0, 1):
        send(h, 0, 0, 0, ALL, "a", 1)
        send(h, 1, 0, 0, ALL, "a", -1)
    for h in (0, 1):
        send(h, 4, 0, 0, ALL, "b", 1)
        send(h, 5, 0, 0, ALL, "b", -1)
    for c in later:
        c.start()
    for h in (0, 1):
        recv(h, 0, -1, 0, ALL)
        send(h, 2, -1, 0, LO, "a", 1)
        send(h, 6, -1, 0, ALL, "b", 1)
        send(h, 7, -1, 0, ALL, "b", -1)
        recv(h, 1, 1, 0, ALL)
        send(h, 3, 1, 0, HI, "a", -1)
        send(h, 8, 1, 0, ALL, "b", 1)
        send(h, 9, 1, 0, ALL, "b", -1)

    def onward(aoff):
        i = LANE_OF[aoff]
        for h in (0, 1):
            recv(h, 4 + 2 * i, aoff, -1, ALL)
            send(h, 12 + 2 * i, aoff, -1, LO, "b", 1)
            recv(h, 5 + 2 * i, aoff, 1, ALL)
            send(h, 13 + 2 * i, aoff, 1, HI, "b", -1)

    onward(0)
    for h in (0, 1):
        recv(h, 2, 2, 0, LO)
        recv(h, 3, 2, 0, HI)
        send(h, 10, 2, 0, ALL, "b", 1)
        send(h, 11, 2, 0, ALL, "b", -1)
    onward(-1)
    onward(1)
    onward(2)

    for c in later:
        c.wait_recv()
    cols = pltpu.make_async_copy(cbuf, csm, smem_sem)
    cols.start()
    for l in range(4):
        base = l * 256 + 224
        prod_hi[base : base + 32, :] = jnp.zeros((32, 512), jnp.bfloat16)
        prod_lo[base : base + 32, :] = jnp.zeros((32, 512), jnp.bfloat16)
    cols.wait()

    for h in (0, 1):
        for aoff in (0, -1, 1, 2):
            i = LANE_OF[aoff]
            recv(h, 12 + 2 * i, aoff, 2, LO)
            recv(h, 13 + 2 * i, aoff, 2, HI)

    left = lax.broadcasted_iota(jnp.int32, (64, 128), 1) < 64
    target = lax.broadcasted_iota(jnp.int32, (128, 256), 0)

    def row_product(r):
        def one_layer(l, carry):
            for kk in range(7):
                col = csm[l, r // 4, r % 4, kk]
                block_p = pall[col // 8, col % 8]
                even_odd = abuf[l, r, kk]
                odd_even = jnp.concatenate([even_odd[:, 64:], even_odd[:, :64]], axis=1)
                zero = jnp.zeros((64, 128), jnp.bfloat16)
                weights = jnp.concatenate(
                    [
                        jnp.where(left, jnp.concatenate([even_odd, odd_even], axis=0), zero),
                        jnp.where(left, zero, jnp.concatenate([odd_even, even_odd], axis=0)),
                    ],
                    axis=0,
                )
                prod = lax.dot_general(
                    block_p, weights, (((1,), (1,)), ((), ())), preferred_element_type=jnp.float32
                )
                moved = pltpu.roll(prod, ROWS - 4, 0)
                base = pl.multiple_of(l * 256 + kk * 32, 32)
                for cp in range(4):
                    part = prod[28 * cp : 28 * cp + 32] if cp % 2 == 0 else moved[28 * cp - 4 : 28 * cp + 28]
                    hi = part.astype(jnp.bfloat16)
                    lo = (part - hi.astype(jnp.float32)).astype(jnp.bfloat16)
                    prod_hi[pl.ds(base, 32), cp * 128 : cp * 128 + 128] = hi
                    prod_lo[pl.ds(base, 32), cp * 128 : cp * 128 + 128] = lo
            return carry

        lax.fori_loop(0, 4, one_layer, 0)
        total = jnp.zeros((128, 512), jnp.float32)
        for l in range(4):
            s = sbuf[l, r]
            lanes = jnp.concatenate([s[0:1], s[1:2]], axis=1)
            chosen = jnp.where(lanes == target, 1.0, 0.0).astype(jnp.bfloat16)
            total += jnp.dot(chosen, prod_hi[l * 256 : l * 256 + 256], preferred_element_type=jnp.float32)
            total += jnp.dot(chosen, prod_lo[l * 256 : l * 256 + 256], preferred_element_type=jnp.float32)
        return total.astype(jnp.bfloat16)

    def give(d, r):
        return remote(obuf.at[d], out.at[j], os.at[d], orr.at[d], dev(y, x, r))

    def one_row(d, carry):
        r = lax.rem(j + d, 8)
        obuf[d] = row_product(r)
        give(d, r).start()
        return carry

    lax.fori_loop(1, 8, one_row, 0)
    out[j] = row_product(j)

    for c in column + later + sent:
        c.wait_send()
    for d in range(1, 8):
        give(d, lax.rem(j + d, 8)).wait()


def per_device(a_blocks, a_cols, p_blocks, slots):
    pt = p_blocks.reshape(28, 64, 8, 4, 2).transpose(2, 3, 0, 4, 1).reshape(8, ROWS, 128)
    a = a_blocks.reshape(4, 7, 32, 128)
    s = jnp.pad(slots, ((0, 0), (0, 1), (0, 4)), constant_values=-1).reshape(4, 2, 128)
    s = jnp.pad(s, ((0, 0), (0, 6), (0, 0)), constant_values=-1)
    cols = jnp.pad(a_cols, ((0, 0), (0, 121)))
    dma = pltpu.SemaphoreType.DMA
    any_ = pl.BlockSpec(memory_space=pl.ANY)
    got = pl.pallas_call(
        kernel,
        out_shape=jax.ShapeDtypeStruct((8, 128, 512), jnp.bfloat16),
        in_specs=[any_, any_, any_, any_],
        out_specs=pl.BlockSpec(memory_space=pltpu.VMEM),
        scratch_shapes=[
            pltpu.VMEM((16, 8, ROWS, 128), jnp.bfloat16),
            pltpu.VMEM((4, 8, 7, 32, 128), jnp.bfloat16),
            pltpu.VMEM((4, 8, 8, 128), jnp.int32),
            pltpu.VMEM((4, 2, 4, 128), jnp.int32),
            pltpu.SMEM((4, 2, 4, 128), jnp.int32),
            pltpu.VMEM((1024, 512), jnp.bfloat16),
            pltpu.VMEM((1024, 512), jnp.bfloat16),
            pltpu.VMEM((8, 128, 512), jnp.bfloat16),
            dma((8,)), dma((8,)), dma((8,)), dma((8,)), dma((8,)), dma((8,)), dma((8,)), dma((8,)),
            dma((4,)), dma((2, 20)), dma((2, 20)), dma((8,)), dma((8,)), dma,
        ],
        compiler_params=pltpu.CompilerParams(
            collective_id=0, has_side_effects=True, vmem_limit_bytes=40 * 2**20
        ),
        name="column_split",
    )(pt, a, s, cols)
    got = got.reshape(8, 128, 4, 2, 2, 32).transpose(1, 5, 4, 0, 2, 3)
    return got.reshape(1, 128, 4096)


def solution(mesh):
    placed = (
        P("grid", "layer", None),
        P("grid", "layer"),
        P(("grid", "layer"), None, None),
        P("grid", "layer", None),
    )
    return jax.shard_map(
        per_device,
        mesh=mesh,
        in_specs=placed,
        out_specs=P(("grid", "layer"), None, None),
        check_vma=False,
    )
```

time: 237 us -> 64.2 us (0.27)
  waiting for transfers between devices: 95.2 us -> 0 us
  local copies, waits for them, and re-layouts: 72 us -> 8.72 us
  Pallas kernels: 0 us -> 55.2 us
  other arithmetic: 28.8 us -> 0 us
  between operations: 13.4 us -> 0.06 us
  matrix products: 13.1 us -> 0 us
  starting transfers between devices: 12.5 us -> 0 us
    all_gather x1 -> x0, waiting for transfers between devices: 89.2 us -> none  [per_device(): gathered = lax.all_gather(p_blocks, ('grid', 'layer'), axis=0, tiled=True)]
    pallas_call x0 -> x1, Pallas kernels: none -> 55.2 us  [per_device(): pl.pallas_call(kernel, out_shape=jax.ShapeDtypeStruct((8, 128, 512), jnp....]
    gather x3 -> x0, local copies, waits for them, and re-layouts: 42.6 us -> none  [one_row(): jnp.take(table, index_row, axis=0).reshape(count, PROLONG_BLOCKS, BS, BS)]
    scatter-add x1 -> x0, other arithmetic: 27.4 us -> none  [one_row(): jax.ops.segment_sum(flipped.reshape(count * PROLONG_BLOCKS, BS * BS), slo...]
    reshape x3 -> x5, local copies, waits for them, and re-layouts: 22.2 us -> 2.83 us  [the longest x1 1.31 us: per_device(): return got.reshape(1, 128, 4096)]
    dot_general x1 -> x0, matrix products: 13.1 us -> none  [one_row(): jnp.einsum('kmbc,kab->kmca', right, left, preferred_element_type=jnp.floa...]
    all_to_all x3 -> x0, starting transfers between devices: 12.5 us -> none  [the longest x1 4.7 us: per_device(): lax.all_to_all(a_cols, 'layer', split_axis=0, concat_axis=1, tiled=True)]
    all_to_all x3 -> x0, waiting for transfers between devices: 5.38 us -> none  [the longest x1 3.92 us: per_device(): lax.all_to_all(a_blocks, 'layer', split_axis=0, concat_axis=1, tiled=True)]
  transfers between devices with their start and end apart: 4 -> 0, of which waited for: 3 -> 0; matrix products, arithmetic and copies ran while one was open for 3% -> 0% of each run, Pallas kernels for 0% -> 0%
where the time goes in v1:
time: 64.2 us; the launch traced here: 64 us
  Pallas kernels  55.2 us (86%)
  local copies, waits for them, and re-layouts  8.72 us (14%)
    pallas_call x1, Pallas kernels, per_device(): pl.pallas_call(kernel, out_shape=jax.ShapeDtypeStruct((8, 128, 512), jnp....  55.2 us
    unnamed x4, local copies, waits for them, and re-layouts  2.13 us
    transpose x1, local copies, waits for them, and re-layouts, per_device(): p_blocks.reshape(28, 64, 8, 4, 2).transpose(2, 3, 0, 4, 1)  1.32 us
    reshape x1, local copies, waits for them, and re-layouts, per_device(): return got.reshape(1, 128, 4096)  1.31 us

profile of v1, /device:TPU:1, one launch (start us, length us, event | category | flops | bytes accessed | tf_op | source)
XLA Modules:
  0.0 64.0 jit_solution(15454134107750100536)
XLA Ops:
  0.0 0.7 %pad.14.col_src = s32[4,128]{1,0:T(4,128)S(1)} pad(s32[4,7]{1,0:T(4,128)} %param.5, s32[]{:T(128)} %constant.1.clone.1), padding=0_0x0_121 | pad | bytes 2164 | tf_op jit(solution)/shard_map/jit(_pad)/pad | solution.py:215
  0.7 0.7 %copy.16 = s32[4,7,28]{2,1,0:T(8,128)S(1)} copy(s32[4,7,28]{2,0,1:T(4,128)} %param.7) | data formatting | bytes 6272
  1.4 0.1 reshape.21
  1.5 1.2 %reshape.20 = bf16[4,7,32,128]{3,2,0,1:T(8,128)(2,1)S(1)} reshape(bf16[4,7,4096]{2,0,1:T(4,128)(2,1)} %param.4) | data formatting | bytes 458752 | tf_op jit(solution)/shard_map/reshape | solution.py:212
  2.7 0.0 copy-start
  2.7 0.9 %copy-done = bf16[1,28,4096]{2,1,0:T(8,128)(2,1)S(1)} copy-done((bf16[1,28,4096]{2,1,0:T(8,128)(2,1)S(1)}, bf16[1,28,4096]{2,1,0:T(8,128)(2,1)}, u32[]{:S(2)}) %copy-start) | copy-done | bytes 229400
  3.6 0.5 copy.9
  4.1 1.3 %copy.10 = bf16[8,4,28,2,64]{4,3,2,1,0:T(2,128)(2,1)S(1)} copy(bf16[8,4,28,2,64]{2,3,1,0,4:T(2,128)(2,1)S(1)} %bitcast.9) | data formatting | bytes 458752 | tf_op jit(solution)/shard_map/transpose | solution.py:211
  5.5 0.2 reshape.19.src
  5.7 55.2 %column_split.1 = bf16[8,128,512]{2,1,0:T(8,128)(2,1)S(1)} custom-call(bf16[8,112,128]{2,1,0:T(8,128)(2,1)S(1)} %reshape.19.src, bf16[4,7,32,128]{3,2,1,0:T(8,128)(2,1)S(1)} %copy.12.a_src, s32[4,8,128]{2,1,0:T(8,128)S(1)} %pad.13.slot_src, s32[4,128]{1,0:T(4,128)S(1)} %pad.14.col_src), custom_call_target="tpu_custom_call" | custom-call | tf_op jit(solution)/shard_map/column_split/pallas_call | solution.py:218
  60.9 0.7 %copy.13 = bf16[8,128,512]{1,2,0:T(8,128)(2,1)S(1)} copy(bf16[8,128,512]{2,1,0:T(8,128)(2,1)S(1)} %column_split.1) | data formatting | bytes 2097152 | tf_op jit(solution)/shard_map/column_split/pallas_call | solution.py:218
  61.6 1.1 %copy.14 = bf16[128,32,2,8,4,2]{0,5,4,3,2,1:T(2,128)(2,1)S(1)} copy(bf16[128,32,2,8,4,2]{0,1,2,5,4,3:T(8,128)(2,1)S(1)} %bitcast.10) | data formatting | bytes 2097152 | tf_op jit(solution)/shard_map/transpose | solution.py:240
  62.7 1.3 %copy.15 = bf16[1,128,4096]{2,1,0:T(8,128)(2,1)} copy(bf16[1,128,4096]{1,2,0:T(8,128)(2,1)S(1)} %bitcast.11) | data formatting | bytes 2097152 | tf_op jit(solution)/shard_map/reshape | solution.py:241
  (3 shorter events, 0.0 us)
Async XLA Ops:
  2.7 1.0 %copy-start = (bf16[1,28,4096]{2,1,0:T(8,128)(2,1)S(1)}, bf16[1,28,4096]{2,1,0:T(8,128)(2,1)}, u32[]{:S(2)}) copy-start(bf16[1,28,4096]{2,1,0:T(8,128)(2,1)} %param.6) | copy-start | bytes 688132

commit v2 on v0

v2 whole, which is shorter than its diff:
```python
import jax
import jax.numpy as jnp
from jax import lax
from jax.experimental import pallas as pl
from jax.experimental.pallas import tpu as pltpu
from jax.sharding import PartitionSpec as P

MESH = pl.DeviceIdType.MESH
ROWS = 112
ALL, LO, HI = (0, 2), (0, 1), (1, 1)
ORDER = {0: 0, -1: 1, 1: 2, 2: 3}
QUARTERS = (0, 1, 3, 2)


def place():
    g, l = lax.axis_index("grid"), lax.axis_index("layer")
    return g // 8, (g // 2) % 4, (g % 2) * 4 + l


def dev(y, x, j):
    return ((y * 4 + x) * 2 + j // 4, j % 4)


def m4(v):
    return lax.rem(v + 4, 4)


def columns_out(tiles):
    lane = lax.broadcasted_iota(jnp.int32, tiles[0].shape, 1)
    for i in range(5):
        d, up = 2 << i, (lane & (2 << i)) != 0
        swapped = list(tiles)
        for t in range(32):
            if not t & (1 << i):
                low, high = tiles[t], tiles[t | (1 << i)]
                swapped[t] = jnp.where(up, pltpu.roll(high, d, 1), low)
                swapped[t | (1 << i)] = jnp.where(up, high, pltpu.roll(low, 128 - d, 1))
        tiles = swapped
    top, bottom = (lane & 64) != 0, (lane & 1) != 0
    done = []
    for v in tiles:
        moved = jnp.where(top, pltpu.roll(v, 63, 1), pltpu.roll(v, 65, 1))
        done.append(jnp.where(top == bottom, v, moved))
    return done


def kernel(
    p_raw, a_raw, slot_raw, col_src, out,
    praw, araw, sraw, pf, pt, af, amine, imine,
    pall, abuf, ibuf, cbuf, csm, wbuf, oh, prod_hi, prod_lo, obuf,
    ls, zs, zr, as_, ar, is_, ir, cs, cr, ss, rs, rl_, os, orr, smem_sem,
):
    y, x, j = place()
    q, z, core = y * 4 + x, j // 2, j % 2
    half, layer = j // 4, j % 4
    part_of_j = layer * 2 + half
    partner = j + 1 - 2 * core
    xs = {0: x, 1: m4(x + 1), 2: m4(x + 2), -1: m4(x - 1)}
    ys = {0: y, 1: m4(y + 1), 2: m4(y + 2), -1: m4(y - 1)}
    beside = {(0, 1): dev(y, xs[1], j), (0, -1): dev(y, xs[-1], j), (1, 1): dev(ys[1], x, j), (1, -1): dev(ys[-1], x, j)}
    chip = {e: m4(z + e) for e in range(4)}

    def in_column(t):
        return (q * 2 + t // 4, t % 4)

    targets = [in_column(lax.rem(j + d, 8)) for d in range(1, 8)]
    barrier = pltpu.get_barrier_semaphore()
    for to in targets + list(beside.values()):
        pl.semaphore_signal(barrier, inc=1, device_id=to, device_id_type=MESH)
    loads = [
        pltpu.make_async_copy(p_raw, praw, ls.at[0]),
        pltpu.make_async_copy(a_raw, araw, ls.at[1]),
        pltpu.make_async_copy(slot_raw, sraw, ls.at[2]),
        pltpu.make_async_copy(col_src, cbuf.at[part_of_j], ls.at[3]),
    ]
    for c in loads:
        c.start()

    def remote(s, d, ssem, rsem, to):
        return pltpu.make_async_remote_copy(
            src_ref=s, dst_ref=d, send_sem=ssem, recv_sem=rsem, device_id=to, device_id_type=MESH
        )

    def take(ref, sem):
        pltpu.make_async_copy(ref, ref, sem).wait()

    loads[0].wait()
    for m in (0, 8, 16, 24):
        rows = min(8, 28 - m)
        tiles = []
        for t in range(32):
            v = praw[m : m + rows, t * 128 : t * 128 + 128].astype(jnp.float32)
            tiles.append(v if rows == 8 else jnp.concatenate([v, v], axis=0))
        for t, v in enumerate(columns_out(tiles)):
            at = (t % 4) * 28 + m
            pf[t // 4, at : at + rows, :] = v[:rows]
    for t in range(8):
        pt[t] = pf[t].astype(jnp.bfloat16)
    pall[q, j] = pt[j]
    pl.semaphore_wait(barrier, 11)

    remote(pt.at[partner], pall.at[q, j], zs, zr.at[0], in_column(partner)).start()
    for e in (1, 3, 2):
        for c in (0, 1):
            t = 2 * m4(z - e) + c
            remote(pt.at[t], pall.at[q, j], zs, zr.at[e], in_column(t)).start()

    def lead(e):
        return 0 if e in (0, 3) else 1

    def spot(e, aoff, boff, rows):
        if lead(e) == 0:
            n = ys[boff] * 4 + xs[aoff]
        else:
            n = ys[aoff] * 4 + xs[boff]
        return pall.at[n, pl.ds(2 * chip[e] + rows[0], rows[1])]

    def send(e, sem, aoff, boff, rows, axis, step):
        ref = spot(e, aoff, boff, rows)
        to = beside[(lead(e) if axis == "a" else 1 - lead(e), step)]
        remote(ref, ref, ss, sem, to).start()

    def both(e, ident, aoff):
        send(e, rs.at[e, ident], aoff, 0, ALL, "b", 1)
        send(e, rs.at[e, ident + 1], aoff, 0, ALL, "b", -1)

    def first(e):
        if e == 0:
            take(pall.at[q, partner], zr.at[0])
        else:
            take(pall.at[q, pl.ds(2 * chip[e], 2)], zr.at[e])
        send(e, rs.at[e, 0], 0, 0, ALL, "a", 1)
        send(e, rs.at[e, 1], 0, 0, ALL, "a", -1)
        both(e, 4, 0)

    def second(e):
        take(spot(e, -1, 0, ALL), rs.at[e, 0])
        send(e, rs.at[e, 2], -1, 0, LO, "a", 1)
        both(e, 6, -1)
        take(spot(e, 1, 0, ALL), rs.at[e, 1])
        send(e, rs.at[e, 2], 1, 0, HI, "a", -1)
        both(e, 8, 1)

    def opposite(e):
        take(spot(e, 2, 0, ALL), rs.at[e, 2])
        both(e, 10, 2)

    def onward(e, aoff):
        i = ORDER[aoff]
        take(spot(e, aoff, -1, ALL), rs.at[e, 4 + 2 * i])
        send(e, rl_, aoff, -1, LO, "b", 1)
        take(spot(e, aoff, 1, ALL), rs.at[e, 5 + 2 * i])
        send(e, rl_, aoff, 1, HI, "b", -1)

    first(0)

    loads[1].wait()
    for kk in range(7):
        for t in range(32):
            af[kk, pl.ds(t, 4, stride=32), :] = araw[kk, :, t * 128 : t * 128 + 128].astype(jnp.float32)
    for kk in range(7):
        for r in range(4):
            amine[r, kk] = af[kk, 32 * r : 32 * r + 32, :].astype(jnp.bfloat16)
    loads[2].wait()
    none = jnp.full((4, 4), -1, jnp.int32)
    for h in (0, 1):
        pieces = []
        for kk in range(4 * h, 4 * h + 4):
            pieces += [sraw[kk], none] if kk < 7 else [jnp.full((4, 32), -1, jnp.int32)]
        imine[h] = jnp.concatenate(pieces, axis=1)
    loads[3].wait()

    def a_part(t):
        return abuf.at[t % 4, pl.ds((t // 4) * 4, 4)]

    a_own = abuf.at[layer, pl.ds(half * 4, 4)]
    own = [pltpu.make_async_copy(amine, a_own, ls.at[4]), pltpu.make_async_copy(imine, ibuf.at[part_of_j], ls.at[5])]
    for c in own:
        c.start()
    a_from = {e: 2 * chip[e] + core for e in (1, 2, 3)}
    for e in (2, 1, 3):
        remote(amine, a_own, as_.at[0], ar.at[e], in_column(2 * m4(z - e) + core)).start()
    remote(amine, a_own, as_.at[1], ar.at[0], in_column(partner)).start()
    for to in targets:
        remote(imine, ibuf.at[part_of_j], is_, ir, to).start()
        remote(cbuf.at[part_of_j], cbuf.at[part_of_j], cs, cr, to).start()

    def a_step(e):
        ref = a_part(a_from[e])
        take(ref, ar.at[e])
        remote(ref, ref, as_.at[1], ar.at[0], in_column(partner)).start()

    for e in QUARTERS[1:]:
        first(e)
    for l in range(4):
        base = l * 256 + 224
        prod_hi[base : base + 32, :] = jnp.zeros((32, 512), jnp.bfloat16)
        prod_lo[base : base + 32, :] = jnp.zeros((32, 512), jnp.bfloat16)
    for e in QUARTERS:
        second(e)
    for e in QUARTERS:
        onward(e, 0)
    take(ibuf.at[pl.ds(0, 7)], ir)
    take(cbuf.at[pl.ds(0, 7)], cr)
    for c in own:
        c.wait()
    cols = pltpu.make_async_copy(cbuf, csm, smem_sem)
    cols.start()

    target = lax.broadcasted_iota(jnp.int32, (128, 256), 0)

    def choose(r, carry):
        for l in range(4):
            s = [ibuf[l * 2 + r // 4, h, pl.ds(r % 4, 1)] for h in (0, 1)]
            lanes = jnp.concatenate(s, axis=1)
            oh[r, l] = jnp.where(lanes == target, 1.0, 0.0).astype(jnp.bfloat16)
        for n, e in enumerate(QUARTERS):
            pl.when(r == 2 * n)(lambda e=e: opposite(e))
        return carry

    lax.fori_loop(0, 8, choose, 0)
    for e in QUARTERS:
        onward(e, -1)
    a_step(1)
    a_step(3)
    a_step(2)
    take(abuf.at[pl.ds(0, 2)], ar.at[0])

    left = lax.broadcasted_iota(jnp.int32, (64, 128), 1) < 64

    def weigh(r, carry):
        for l in range(4):
            for kk in range(7):
                even_odd = abuf[l, r, kk]
                odd_even = jnp.concatenate([even_odd[:, 64:], even_odd[:, :64]], axis=1)
                zero = jnp.zeros((64, 128), jnp.bfloat16)
                wbuf[l, r, kk, 0:64] = jnp.where(left, jnp.concatenate([even_odd, odd_even], axis=0), zero)
                wbuf[l, r, kk, 64:128] = jnp.where(left, zero, jnp.concatenate([odd_even, even_odd], axis=0))
        for n, e in enumerate(QUARTERS):
            pl.when(r == n)(lambda e=e: onward(e, 1))
            pl.when(r == n + 4)(lambda e=e: onward(e, 2))
        return carry

    lax.fori_loop(0, 8, weigh, 0)
    cols.wait()
    take(pall.at[pl.ds(0, 4)], rl_)

    def row_product(r):
        rh, rl = r // 4, r % 4
        for l in range(4):
            for kk in range(7):
                col = csm[l * 2 + rh, rl, kk]
                prod = lax.dot_general(
                    pall[col // 8, col % 8], wbuf[l, r, kk], (((1,), (1,)), ((), ())),
                    preferred_element_type=jnp.float32,
                )
                moved = pltpu.roll(prod, ROWS - 4, 0)
                base = l * 256 + kk * 32
                for cp in range(4):
                    part = prod[28 * cp : 28 * cp + 32] if cp % 2 == 0 else moved[28 * cp - 4 : 28 * cp + 28]
                    hi = part.astype(jnp.bfloat16)
                    lo = (part - hi.astype(jnp.float32)).astype(jnp.bfloat16)
                    prod_hi[base : base + 32, cp * 128 : cp * 128 + 128] = hi
                    prod_lo[base : base + 32, cp * 128 : cp * 128 + 128] = lo
        total = jnp.zeros((128, 512), jnp.float32)
        for l in range(4):
            total += jnp.dot(oh[r, l], prod_hi[l * 256 : l * 256 + 256], preferred_element_type=jnp.float32)
            total += jnp.dot(oh[r, l], prod_lo[l * 256 : l * 256 + 256], preferred_element_type=jnp.float32)
        return total.astype(jnp.bfloat16)

    def one_row(n, carry):
        p = n // 2
        e = (2 + 2 * (p // 2) + (p // 2 + p) % 2) % 4
        r = 2 * ((z + e) % 4) + (core + 1 + n) % 2
        obuf[n] = row_product(r)

        @pl.when(n < 7)
        def _():
            remote(obuf.at[n], out.at[j], os, orr, in_column(r)).start()

        return carry

    lax.fori_loop(0, 8, one_row, 0)
    out[j] = obuf[7]

    take(pall.at[q, pl.ds(0, 7)], zs)
    take(abuf.at[pl.ds(0, 3), pl.ds(0, 4)], as_.at[0])
    take(abuf.at[pl.ds(0, 2)], as_.at[1])
    take(ibuf.at[pl.ds(0, 7)], is_)
    take(cbuf.at[pl.ds(0, 7)], cs)
    take(pall.at[pl.ds(0, 15)], ss)
    take(obuf.at[pl.ds(0, 7)], os)
    take(out.at[pl.ds(0, 7)], orr)


def per_device(a_blocks, a_cols, p_blocks, slots):
    dma = pltpu.SemaphoreType.DMA
    hbm = pl.BlockSpec(memory_space=pltpu.HBM)
    got = pl.pallas_call(
        kernel,
        out_shape=jax.ShapeDtypeStruct((8, 128, 512), jnp.bfloat16),
        in_specs=[hbm, hbm, hbm, hbm],
        out_specs=pl.BlockSpec(memory_space=pltpu.VMEM),
        scratch_shapes=[
            pltpu.VMEM((28, 4096), jnp.bfloat16),
            pltpu.VMEM((7, 4, 4096), jnp.bfloat16),
            pltpu.VMEM((7, 4, 28), jnp.int32),
            pltpu.VMEM((8, ROWS, 128), jnp.float32),
            pltpu.VMEM((8, ROWS, 128), jnp.bfloat16),
            pltpu.VMEM((7, 128, 128), jnp.float32),
            pltpu.VMEM((4, 7, 32, 128), jnp.bfloat16),
            pltpu.VMEM((2, 4, 128), jnp.int32),
            pltpu.VMEM((16, 8, ROWS, 128), jnp.bfloat16),
            pltpu.VMEM((4, 8, 7, 32, 128), jnp.bfloat16),
            pltpu.VMEM((8, 2, 4, 128), jnp.int32),
            pltpu.VMEM((8, 4, 7), jnp.int32),
            pltpu.SMEM((8, 4, 7), jnp.int32),
            pltpu.VMEM((4, 8, 7, 128, 128), jnp.bfloat16),
            pltpu.VMEM((8, 4, 128, 256), jnp.bfloat16),
            pltpu.VMEM((1024, 512), jnp.bfloat16),
            pltpu.VMEM((1024, 512), jnp.bfloat16),
            pltpu.VMEM((8, 128, 512), jnp.bfloat16),
            dma((6,)), dma, dma((4,)), dma((2,)), dma((4,)), dma, dma, dma, dma,
            dma, dma((4, 12)), dma, dma, dma, dma,
        ],
        compiler_params=pltpu.CompilerParams(
            collective_id=0, has_side_effects=True, vmem_limit_bytes=60 * 2**20
        ),
        name="column_split",
    )(p_blocks[0], a_blocks.transpose(1, 0, 2), slots.transpose(1, 0, 2), a_cols)
    got = got.reshape(8, 128, 4, 2, 2, 32).transpose(1, 5, 4, 0, 2, 3)
    return got.reshape(1, 128, 4096)


def solution(mesh):
    placed = (
        P("grid", "layer", None),
        P("grid", "layer"),
        P(("grid", "layer"), None, None),
        P("grid", "layer", None),
    )
    return jax.shard_map(
        per_device,
        mesh=mesh,
        in_specs=placed,
        out_specs=P(("grid", "layer"), None, None),
        check_vma=False,
    )
```

time: 237 us -> 51.6 us (0.22)
  waiting for transfers between devices: 95.2 us -> 0 us
  local copies, waits for them, and re-layouts: 72 us -> 4.01 us
  Pallas kernels: 0 us -> 47.4 us
  other arithmetic: 28.8 us -> 0 us
  between operations: 13.4 us -> 0.02 us
  matrix products: 13.1 us -> 0 us
  starting transfers between devices: 12.5 us -> 0 us
    all_gather x1 -> x0, waiting for transfers between devices: 89.2 us -> none  [per_device(): gathered = lax.all_gather(p_blocks, ('grid', 'layer'), axis=0, tiled=True)]
    pallas_call x0 -> x1, Pallas kernels: none -> 47.4 us  [per_device(): pl.pallas_call(kernel, out_shape=jax.ShapeDtypeStruct((8, 128, 512), jnp....]
    gather x3 -> x0, local copies, waits for them, and re-layouts: 42.6 us -> none  [one_row(): jnp.take(table, index_row, axis=0).reshape(count, PROLONG_BLOCKS, BS, BS)]
    scatter-add x1 -> x0, other arithmetic: 27.4 us -> none  [one_row(): jax.ops.segment_sum(flipped.reshape(count * PROLONG_BLOCKS, BS * BS), slo...]
    reshape x3 -> x1, local copies, waits for them, and re-layouts: 22.2 us -> 1.31 us  [per_device(): return got.reshape(1, 128, 4096)]
    dot_general x1 -> x0, matrix products: 13.1 us -> none  [one_row(): jnp.einsum('kmbc,kab->kmca', right, left, preferred_element_type=jnp.floa...]
    all_to_all x3 -> x0, starting transfers between devices: 12.5 us -> none  [the longest x1 4.7 us: per_device(): lax.all_to_all(a_cols, 'layer', split_axis=0, concat_axis=1, tiled=True)]
    all_to_all x3 -> x0, waiting for transfers between devices: 5.38 us -> none  [the longest x1 3.92 us: per_device(): lax.all_to_all(a_blocks, 'layer', split_axis=0, concat_axis=1, tiled=True)]
  transfers between devices with their start and end apart: 4 -> 0, of which waited for: 3 -> 0; matrix products, arithmetic and copies ran while one was open for 3% -> 0% of each run, Pallas kernels for 0% -> 0%
where the time goes in v2:
time: 51.6 us; the launch traced here: 51.4 us
  Pallas kernels  47.4 us (92%)
  local copies, waits for them, and re-layouts  4.01 us (8%)
    pallas_call x1, Pallas kernels, per_device(): pl.pallas_call(kernel, out_shape=jax.ShapeDtypeStruct((8, 128, 512), jnp....  47.4 us
    pallas_call x1, local copies, waits for them, and re-layouts, per_device(): pl.pallas_call(kernel, out_shape=jax.ShapeDtypeStruct((8, 128, 512), jnp....  1.62 us
    reshape x1, local copies, waits for them, and re-layouts, per_device(): return got.reshape(1, 128, 4096)  1.31 us
    transpose x1, local copies, waits for them, and re-layouts, per_device(): got = got.reshape(8, 128, 4, 2, 2, 32).transpose(1, 5, 4, 0, 2, 3)  1.08 us

profile of v2, /device:TPU:1, one launch (start us, length us, event | category | flops | bytes accessed | tf_op | source)
XLA Modules:
  0.0 51.4 jit_solution(10031716593605946068)
XLA Ops:
  0.0 47.4 %column_split.1 = bf16[8,128,512]{2,1,0:T(8,128)(2,1)} custom-call(bf16[28,4096]{1,0:T(8,128)(2,1)} %bitcast.9, bf16[7,4,4096]{2,1,0:T(4,128)(2,1)} %bitcast.10, s32[7,4,28]{2,1,0:T(4,128)} %bitcast.11, s32[4,7]{1,0:T(4,128)} %col_src.1), custom_call_target="tpu_custom_call" | custom-call | tf_op jit(solution)/shard_map/column_split/pallas_call | solution.py:299
  47.4 1.6 %copy.6 = bf16[8,128,512]{1,2,0:T(8,128)(2,1)S(1)} copy(bf16[8,128,512]{2,1,0:T(8,128)(2,1)} %column_split.1) | data formatting | bytes 2097152 | tf_op jit(solution)/shard_map/column_split/pallas_call | solution.py:299
  49.0 1.1 %copy.7 = bf16[128,32,2,8,4,2]{0,5,4,3,2,1:T(2,128)(2,1)S(1)} copy(bf16[128,32,2,8,4,2]{0,1,2,5,4,3:T(8,128)(2,1)S(1)} %bitcast.7) | data formatting | bytes 2097152 | tf_op jit(solution)/shard_map/transpose | solution.py:331
  50.1 1.3 %copy.8 = bf16[1,128,4096]{2,1,0:T(8,128)(2,1)} copy(bf16[1,128,4096]{1,2,0:T(8,128)(2,1)S(1)} %bitcast.8) | data formatting | bytes 2097152 | tf_op jit(solution)/shard_map/reshape | solution.py:332

commit v3 on v2

--- a/solution.py
+++ b/solution.py
@@ -47,7 +47,7 @@
 def kernel(
     p_raw, a_raw, slot_raw, col_src, out,
     praw, araw, sraw, pf, pt, af, amine, imine,
-    pall, abuf, ibuf, cbuf, csm, wbuf, oh, prod_hi, prod_lo, obuf,
+    pall, abuf, ibuf, cbuf, csm, wbuf, oh, prod_hi, prod_lo, of, obuf,
     ls, zs, zr, as_, ar, is_, ir, cs, cr, ss, rs, rl_, os, orr, smem_sem,
 ):
     y, x, j = place()
@@ -266,7 +266,13 @@
         for l in range(4):
             total += jnp.dot(oh[r, l], prod_hi[l * 256 : l * 256 + 256], preferred_element_type=jnp.float32)
             total += jnp.dot(oh[r, l], prod_lo[l * 256 : l * 256 + 256], preferred_element_type=jnp.float32)
-        return total.astype(jnp.bfloat16)
+        for cp in range(4):
+            turned = total[:, cp * 128 : cp * 128 + 128].T
+            for c0 in (0, 1):
+                for a0 in (0, 1):
+                    n = 64 * c0 + 32 * a0
+                    of[pl.ds(8 * a0 + 2 * cp + c0, 32, stride=16), :] = turned[n : n + 32]
+        return of[...].reshape(64, 8, 128).astype(jnp.bfloat16)
 
     def one_row(n, carry):
         p = n // 2
@@ -276,12 +282,12 @@
 
         @pl.when(n < 7)
         def _():
-            remote(obuf.at[n], out.at[j], os, orr, in_column(r)).start()
+            remote(obuf.at[n], out.at[:, j], os, orr, in_column(r)).start()
 
         return carry
 
     lax.fori_loop(0, 8, one_row, 0)
-    out[j] = obuf[7]
+    out[:, j] = obuf[7]
 
     take(pall.at[q, pl.ds(0, 7)], zs)
     take(abuf.at[pl.ds(0, 3), pl.ds(0, 4)], as_.at[0])
@@ -290,7 +296,7 @@
     take(cbuf.at[pl.ds(0, 7)], cs)
     take(pall.at[pl.ds(0, 15)], ss)
     take(obuf.at[pl.ds(0, 7)], os)
-    take(out.at[pl.ds(0, 7)], orr)
+    take(out.at[:, pl.ds(0, 7)], orr)
 
 
 def per_device(a_blocks, a_cols, p_blocks, slots):
@@ -298,7 +304,7 @@
     hbm = pl.BlockSpec(memory_space=pltpu.HBM)
     got = pl.pallas_call(
         kernel,
-        out_shape=jax.ShapeDtypeStruct((8, 128, 512), jnp.bfloat16),
+        out_shape=jax.ShapeDtypeStruct((64, 8, 8, 128), jnp.bfloat16),
         in_specs=[hbm, hbm, hbm, hbm],
         out_specs=pl.BlockSpec(memory_space=pltpu.VMEM),
         scratch_shapes=[
@@ -319,7 +325,8 @@
             pltpu.VMEM((8, 4, 128, 256), jnp.bfloat16),
             pltpu.VMEM((1024, 512), jnp.bfloat16),
             pltpu.VMEM((1024, 512), jnp.bfloat16),
-            pltpu.VMEM((8, 128, 512), jnp.bfloat16),
+            pltpu.VMEM((512, 128), jnp.float32),
+            pltpu.VMEM((8, 64, 8, 128), jnp.bfloat16),
             dma((6,)), dma, dma((4,)), dma((2,)), dma((4,)), dma, dma, dma, dma,
             dma, dma((4, 12)), dma, dma, dma, dma,
         ],
@@ -328,8 +335,7 @@
         ),
         name="column_split",
     )(p_blocks[0], a_blocks.transpose(1, 0, 2), slots.transpose(1, 0, 2), a_cols)
-    got = got.reshape(8, 128, 4, 2, 2, 32).transpose(1, 5, 4, 0, 2, 3)
-    return got.reshape(1, 128, 4096)
+    return got.reshape(4096, 128).T[None]
 
 
 def solution(mesh):

time: 51.6 us -> 49.9 us (0.967)
  local copies, waits for them, and re-layouts: 4.01 us -> 2.27 us
    pallas_call x1 -> x0, local copies, waits for them, and re-layouts: 1.62 us -> none  [per_device(): pl.pallas_call(kernel, out_shape=jax.ShapeDtypeStruct((8, 128, 512), jnp....]
    transpose x1 -> x0, local copies, waits for them, and re-layouts: 1.08 us -> none  [per_device(): got = got.reshape(8, 128, 4, 2, 2, 32).transpose(1, 5, 4, 0, 2, 3)]
    reshape x1, local copies, waits for them, and re-layouts: 1.31 us -> 2.27 us  [per_device(): return got.reshape(4096, 128).T[None]]
where the time goes in v3:
time: 49.9 us; the launch traced here: 49.8 us
  Pallas kernels  47.5 us (95%)
  local copies, waits for them, and re-layouts  2.27 us (5%)
    pallas_call x1, Pallas kernels, per_device(): pl.pallas_call(kernel, out_shape=jax.ShapeDtypeStruct((64, 8, 8, 128), jn...  47.5 us
    reshape x1, local copies, waits for them, and re-layouts, per_device(): return got.reshape(4096, 128).T[None]  2.27 us

profile of v3, /device:TPU:1, one launch (start us, length us, event | category | flops | bytes accessed | tf_op | source)
XLA Modules:
  0.0 49.8 jit_solution(373416356863831886)
XLA Ops:
  0.0 47.5 %column_split.1 = bf16[64,8,8,128]{3,2,1,0:T(8,128)(2,1)} custom-call(bf16[28,4096]{1,0:T(8,128)(2,1)} %bitcast.8, bf16[7,4,4096]{2,1,0:T(4,128)(2,1)} %bitcast.9, s32[7,4,28]{2,1,0:T(4,128)} %bitcast.10, s32[4,7]{1,0:T(4,128)} %col_src.1), custom_call_target="tpu_custom_call" | custom-call | tf_op jit(solution)/shard_map/column_split/pallas_call | solution.py:305
  47.5 2.3 %copy.5 = bf16[4096,128]{0,1:T(8,128)(2,1)} copy(bf16[4096,128]{1,0:T(8,128)(2,1)} %bitcast.7) | data formatting | bytes 2097152 | tf_op jit(solution)/shard_map/reshape | solution.py:338

commit v4 on v3

--- a/solution.py
+++ b/solution.py
@@ -46,9 +46,9 @@
 
 def kernel(
     p_raw, a_raw, slot_raw, col_src, out,
-    praw, araw, sraw, pf, pt, af, amine, imine,
-    pall, abuf, ibuf, cbuf, csm, wbuf, oh, prod_hi, prod_lo, of, obuf,
-    ls, zs, zr, as_, ar, is_, ir, cs, cr, ss, rs, rl_, os, orr, smem_sem,
+    praw, araw, sraw, craw, pf, pt, af, amine, imine,
+    pall, abuf, ibuf, csm, wbuf, oh, prod_hi, prod_lo, of, obuf,
+    ls, zs, zr, as_, ar, is_, ir, ss, rs, rl_, os, orr, smem_sem,
 ):
     y, x, j = place()
     q, z, core = y * 4 + x, j // 2, j % 2
@@ -71,7 +71,7 @@
         pltpu.make_async_copy(p_raw, praw, ls.at[0]),
         pltpu.make_async_copy(a_raw, araw, ls.at[1]),
         pltpu.make_async_copy(slot_raw, sraw, ls.at[2]),
-        pltpu.make_async_copy(col_src, cbuf.at[part_of_j], ls.at[3]),
+        pltpu.make_async_copy(col_src, craw, ls.at[3]),
     ]
     for c in loads:
         c.start()
@@ -162,13 +162,13 @@
         for r in range(4):
             amine[r, kk] = af[kk, 32 * r : 32 * r + 32, :].astype(jnp.bfloat16)
     loads[2].wait()
+    loads[3].wait()
     none = jnp.full((4, 4), -1, jnp.int32)
     for h in (0, 1):
         pieces = []
         for kk in range(4 * h, 4 * h + 4):
-            pieces += [sraw[kk], none] if kk < 7 else [jnp.full((4, 32), -1, jnp.int32)]
+            pieces += [sraw[kk], none] if kk < 7 else [craw[...], jnp.full((4, 25), -1, jnp.int32)]
         imine[h] = jnp.concatenate(pieces, axis=1)
-    loads[3].wait()
 
     def a_part(t):
         return abuf.at[t % 4, pl.ds((t // 4) * 4, 4)]
@@ -183,7 +183,6 @@
     remote(amine, a_own, as_.at[1], ar.at[0], in_column(partner)).start()
     for to in targets:
         remote(imine, ibuf.at[part_of_j], is_, ir, to).start()
-        remote(cbuf.at[part_of_j], cbuf.at[part_of_j], cs, cr, to).start()
 
     def a_step(e):
         ref = a_part(a_from[e])
@@ -201,10 +200,9 @@
     for e in QUARTERS:
         onward(e, 0)
     take(ibuf.at[pl.ds(0, 7)], ir)
-    take(cbuf.at[pl.ds(0, 7)], cr)
     for c in own:
         c.wait()
-    cols = pltpu.make_async_copy(cbuf, csm, smem_sem)
+    cols = pltpu.make_async_copy(ibuf.at[:, 1], csm, smem_sem)
     cols.start()
 
     target = lax.broadcasted_iota(jnp.int32, (128, 256), 0)
@@ -221,37 +219,34 @@
     lax.fori_loop(0, 8, choose, 0)
     for e in QUARTERS:
         onward(e, -1)
+    for e in QUARTERS:
+        onward(e, 1)
     a_step(1)
     a_step(3)
     a_step(2)
-    take(abuf.at[pl.ds(0, 2)], ar.at[0])
+    for e in QUARTERS:
+        onward(e, 2)
 
     left = lax.broadcasted_iota(jnp.int32, (64, 128), 1) < 64
 
-    def weigh(r, carry):
+    def weigh(r):
         for l in range(4):
             for kk in range(7):
                 even_odd = abuf[l, r, kk]
                 odd_even = jnp.concatenate([even_odd[:, 64:], even_odd[:, :64]], axis=1)
                 zero = jnp.zeros((64, 128), jnp.bfloat16)
-                wbuf[l, r, kk, 0:64] = jnp.where(left, jnp.concatenate([even_odd, odd_even], axis=0), zero)
-                wbuf[l, r, kk, 64:128] = jnp.where(left, zero, jnp.concatenate([odd_even, even_odd], axis=0))
-        for n, e in enumerate(QUARTERS):
-            pl.when(r == n)(lambda e=e: onward(e, 1))
-            pl.when(r == n + 4)(lambda e=e: onward(e, 2))
-        return carry
-
-    lax.fori_loop(0, 8, weigh, 0)
+                wbuf[l, kk, 0:64] = jnp.where(left, jnp.concatenate([even_odd, odd_even], axis=0), zero)
+                wbuf[l, kk, 64:128] = jnp.where(left, zero, jnp.concatenate([odd_even, even_odd], axis=0))
+
     cols.wait()
-    take(pall.at[pl.ds(0, 4)], rl_)
 
     def row_product(r):
         rh, rl = r // 4, r % 4
         for l in range(4):
             for kk in range(7):
-                col = csm[l * 2 + rh, rl, kk]
+                col = csm[l * 2 + rh, rl, 96 + kk]
                 prod = lax.dot_general(
-                    pall[col // 8, col % 8], wbuf[l, r, kk], (((1,), (1,)), ((), ())),
+                    pall[col // 8, col % 8], wbuf[l, kk], (((1,), (1,)), ((), ())),
                     preferred_element_type=jnp.float32,
                 )
                 moved = pltpu.roll(prod, ROWS - 4, 0)
@@ -274,18 +269,25 @@
                     of[pl.ds(8 * a0 + 2 * cp + c0, 32, stride=16), :] = turned[n : n + 32]
         return of[...].reshape(64, 8, 128).astype(jnp.bfloat16)
 
-    def one_row(n, carry):
+    def turn(n):
         p = n // 2
         e = (2 + 2 * (p // 2) + (p // 2 + p) % 2) % 4
-        r = 2 * ((z + e) % 4) + (core + 1 + n) % 2
+        return 2 * ((z + e) % 4) + (core + 1 + n) % 2
+
+    def one_row(n, carry):
+        r = turn(n)
         obuf[n] = row_product(r)
 
         @pl.when(n < 7)
         def _():
             remote(obuf.at[n], out.at[:, j], os, orr, in_column(r)).start()
+            weigh(turn(n + 1))
 
         return carry
 
+    take(abuf.at[pl.ds(0, 2)], ar.at[0])
+    weigh(turn(0))
+    take(pall.at[pl.ds(0, 4)], rl_)
     lax.fori_loop(0, 8, one_row, 0)
     out[:, j] = obuf[7]
 
@@ -293,7 +295,6 @@
     take(abuf.at[pl.ds(0, 3), pl.ds(0, 4)], as_.at[0])
     take(abuf.at[pl.ds(0, 2)], as_.at[1])
     take(ibuf.at[pl.ds(0, 7)], is_)
-    take(cbuf.at[pl.ds(0, 7)], cs)
     take(pall.at[pl.ds(0, 15)], ss)
     take(obuf.at[pl.ds(0, 7)], os)
     take(out.at[:, pl.ds(0, 7)], orr)
@@ -311,6 +312,7 @@
             pltpu.VMEM((28, 4096), jnp.bfloat16),
             pltpu.VMEM((7, 4, 4096), jnp.bfloat16),
             pltpu.VMEM((7, 4, 28), jnp.int32),
+            pltpu.VMEM((4, 7), jnp.int32),
             pltpu.VMEM((8, ROWS, 128), jnp.float32),
             pltpu.VMEM((8, ROWS, 128), jnp.bfloat16),
             pltpu.VMEM((7, 128, 128), jnp.float32),
@@ -319,15 +321,14 @@
             pltpu.VMEM((16, 8, ROWS, 128), jnp.bfloat16),
             pltpu.VMEM((4, 8, 7, 32, 128), jnp.bfloat16),
             pltpu.VMEM((8, 2, 4, 128), jnp.int32),
-            pltpu.VMEM((8, 4, 7), jnp.int32),
-            pltpu.SMEM((8, 4, 7), jnp.int32),
-            pltpu.VMEM((4, 8, 7, 128, 128), jnp.bfloat16),
+            pltpu.SMEM((8, 4, 128), jnp.int32),
+            pltpu.VMEM((4, 7, 128, 128), jnp.bfloat16),
             pltpu.VMEM((8, 4, 128, 256), jnp.bfloat16),
             pltpu.VMEM((1024, 512), jnp.bfloat16),
             pltpu.VMEM((1024, 512), jnp.bfloat16),
             pltpu.VMEM((512, 128), jnp.float32),
             pltpu.VMEM((8, 64, 8, 128), jnp.bfloat16),
-            dma((6,)), dma, dma((4,)), dma((2,)), dma((4,)), dma, dma, dma, dma,
+            dma((6,)), dma, dma((4,)), dma((2,)), dma((4,)), dma, dma,
             dma, dma((4, 12)), dma, dma, dma, dma,
         ],
         compiler_params=pltpu.CompilerParams(

time: 49.9 us -> 49.1 us (0.984)
  Pallas kernels: 47.5 us -> 46.7 us
    pallas_call x1, Pallas kernels: 47.5 us -> 46.7 us  [per_device(): pl.pallas_call(kernel, out_shape=jax.ShapeDtypeStruct((64, 8, 8, 128), jn...]
where the time goes in v4:
time: 49.1 us; the launch traced here: 49 us
  Pallas kernels  46.7 us (95%)
  local copies, waits for them, and re-layouts  2.27 us (5%)
    pallas_call x1, Pallas kernels, per_device(): pl.pallas_call(kernel, out_shape=jax.ShapeDtypeStruct((64, 8, 8, 128), jn...  46.7 us
    reshape x1, local copies, waits for them, and re-layouts, per_device(): return got.reshape(4096, 128).T[None]  2.27 us

profile of v4, /device:TPU:1, one launch (start us, length us, event | category | flops | bytes accessed | tf_op | source)
XLA Modules:
  0.0 49.0 jit_solution(12002110660261729711)
XLA Ops:
  0.0 46.7 %column_split.1 = bf16[64,8,8,128]{3,2,1,0:T(8,128)(2,1)} custom-call(bf16[28,4096]{1,0:T(8,128)(2,1)} %bitcast.8, bf16[7,4,4096]{2,1,0:T(4,128)(2,1)} %bitcast.9, s32[7,4,28]{2,1,0:T(4,128)} %bitcast.10, s32[4,7]{1,0:T(4,128)} %col_src.1), custom_call_target="tpu_custom_call" | custom-call | tf_op jit(solution)/shard_map/column_split/pallas_call | solution.py:306
  46.7 2.3 %copy.5 = bf16[4096,128]{0,1:T(8,128)(2,1)} copy(bf16[4096,128]{1,0:T(8,128)(2,1)} %bitcast.7) | data formatting | bytes 2097152 | tf_op jit(solution)/shard_map/reshape | solution.py:339

commit v5 on v4

--- a/solution.py
+++ b/solution.py
@@ -289,7 +289,8 @@
     weigh(turn(0))
     take(pall.at[pl.ds(0, 4)], rl_)
     lax.fori_loop(0, 8, one_row, 0)
-    out[:, j] = obuf[7]
+    last = pltpu.make_async_copy(obuf.at[7], out.at[:, j], smem_sem)
+    last.start()
 
     take(pall.at[q, pl.ds(0, 7)], zs)
     take(abuf.at[pl.ds(0, 3), pl.ds(0, 4)], as_.at[0])
@@ -298,6 +299,7 @@
     take(pall.at[pl.ds(0, 15)], ss)
     take(obuf.at[pl.ds(0, 7)], os)
     take(out.at[:, pl.ds(0, 7)], orr)
+    last.wait()
 
 
 def per_device(a_blocks, a_cols, p_blocks, slots):
@@ -307,7 +309,7 @@
         kernel,
         out_shape=jax.ShapeDtypeStruct((64, 8, 8, 128), jnp.bfloat16),
         in_specs=[hbm, hbm, hbm, hbm],
-        out_specs=pl.BlockSpec(memory_space=pltpu.VMEM),
+        out_specs=hbm,
         scratch_shapes=[
             pltpu.VMEM((28, 4096), jnp.bfloat16),
             pltpu.VMEM((7, 4, 4096), jnp.bfloat16),

time: 49.1 us -> 48.3 us (0.984)
  Pallas kernels: 46.7 us -> 45.8 us
    pallas_call x1, Pallas kernels: 46.7 us -> 45.8 us  [per_device(): pl.pallas_call(kernel, out_shape=jax.ShapeDtypeStruct((64, 8, 8, 128), jn...]
where the time goes in v5:
time: 48.3 us; the launch traced here: 48.1 us
  Pallas kernels  45.8 us (95%)
  local copies, waits for them, and re-layouts  2.27 us (5%)
    pallas_call x1, Pallas kernels, per_device(): pl.pallas_call(kernel, out_shape=jax.ShapeDtypeStruct((64, 8, 8, 128), jn...  45.8 us
    reshape x1, local copies, waits for them, and re-layouts, per_device(): return got.reshape(4096, 128).T[None]  2.27 us

profile of v5, /device:TPU:1, one launch (start us, length us, event | category | flops | bytes accessed | tf_op | source)
XLA Modules:
  0.0 48.1 jit_solution(1220044730281330819)
XLA Ops:
  0.0 45.8 %column_split.1 = bf16[64,8,8,128]{3,2,1,0:T(8,128)(2,1)} custom-call(bf16[28,4096]{1,0:T(8,128)(2,1)} %bitcast.8, bf16[7,4,4096]{2,1,0:T(4,128)(2,1)} %bitcast.9, s32[7,4,28]{2,1,0:T(4,128)} %bitcast.10, s32[4,7]{1,0:T(4,128)} %col_src.1), custom_call_target="tpu_custom_call" | custom-call | tf_op jit(solution)/shard_map/column_split/pallas_call | solution.py:308
  45.9 2.3 %copy.5 = bf16[4096,128]{0,1:T(8,128)(2,1)} copy(bf16[4096,128]{1,0:T(8,128)(2,1)} %bitcast.7) | data formatting | bytes 2097152 | tf_op jit(solution)/shard_map/reshape | solution.py:341

commit v6 on v5

--- a/solution.py
+++ b/solution.py
@@ -161,6 +161,30 @@
     for kk in range(7):
         for r in range(4):
             amine[r, kk] = af[kk, 32 * r : 32 * r + 32, :].astype(jnp.bfloat16)
+    def a_part(t):
+        return abuf.at[t % 4, pl.ds((t // 4) * 4, 4)]
+
+    a_own = abuf.at[layer, pl.ds(half * 4, 4)]
+    own = [pltpu.make_async_copy(amine, a_own, ls.at[4]), pltpu.make_async_copy(imine, ibuf.at[part_of_j], ls.at[5])]
+    own[0].start()
+    a_from = {e: 2 * chip[e] + core for e in (1, 2, 3)}
+    for e in (2, 1, 3):
+        remote(amine, a_own, as_.at[0], ar.at[e], in_column(2 * m4(z - e) + core)).start()
+    remote(amine, a_own, as_.at[1], ar.at[0], in_column(partner)).start()
+
+    def a_step(e):
+        ref = a_part(a_from[e])
+        take(ref, ar.at[e])
+        remote(ref, ref, as_.at[1], ar.at[0], in_column(partner)).start()
+
+    for e in QUARTERS[1:]:
+        first(e)
+    for l in range(4):
+        base = l * 256 + 224
+        prod_hi[base : base + 32, :] = jnp.zeros((32, 512), jnp.bfloat16)
+        prod_lo[base : base + 32, :] = jnp.zeros((32, 512), jnp.bfloat16)
+    second(0)
+    second(1)
     loads[2].wait()
     loads[3].wait()
     none = jnp.full((4, 4), -1, jnp.int32)
@@ -170,33 +194,11 @@
             pieces += [sraw[kk], none] if kk < 7 else [craw[...], jnp.full((4, 25), -1, jnp.int32)]
         imine[h] = jnp.concatenate(pieces, axis=1)
 
-    def a_part(t):
-        return abuf.at[t % 4, pl.ds((t // 4) * 4, 4)]
-
-    a_own = abuf.at[layer, pl.ds(half * 4, 4)]
-    own = [pltpu.make_async_copy(amine, a_own, ls.at[4]), pltpu.make_async_copy(imine, ibuf.at[part_of_j], ls.at[5])]
-    for c in own:
-        c.start()
-    a_from = {e: 2 * chip[e] + core for e in (1, 2, 3)}
-    for e in (2, 1, 3):
-        remote(amine, a_own, as_.at[0], ar.at[e], in_column(2 * m4(z - e) + core)).start()
-    remote(amine, a_own, as_.at[1], ar.at[0], in_column(partner)).start()
+    own[1].start()
     for to in targets:
         remote(imine, ibuf.at[part_of_j], is_, ir, to).start()
-
-    def a_step(e):
-        ref = a_part(a_from[e])
-        take(ref, ar.at[e])
-        remote(ref, ref, as_.at[1], ar.at[0], in_column(partner)).start()
-
-    for e in QUARTERS[1:]:
-        first(e)
-    for l in range(4):
-        base = l * 256 + 224
-        prod_hi[base : base + 32, :] = jnp.zeros((32, 512), jnp.bfloat16)
-        prod_lo[base : base + 32, :] = jnp.zeros((32, 512), jnp.bfloat16)
-    for e in QUARTERS:
-        second(e)
+    second(3)
+    second(2)
     for e in QUARTERS:
         onward(e, 0)
     take(ibuf.at[pl.ds(0, 7)], ir)
@@ -213,12 +215,11 @@
             lanes = jnp.concatenate(s, axis=1)
             oh[r, l] = jnp.where(lanes == target, 1.0, 0.0).astype(jnp.bfloat16)
         for n, e in enumerate(QUARTERS):
-            pl.when(r == 2 * n)(lambda e=e: opposite(e))
+            pl.when(r == n)(lambda e=e: opposite(e))
+            pl.when(r == n + 4)(lambda e=e: onward(e, -1))
         return carry
 
     lax.fori_loop(0, 8, choose, 0)
-    for e in QUARTERS:
-        onward(e, -1)
     for e in QUARTERS:
         onward(e, 1)
     a_step(1)

time: 48.3 us -> 48.2 us (level)
  no operation moved by 1% of the time
where the time goes in v6:
time: 48.2 us; the launch traced here: 48.1 us
  Pallas kernels  45.8 us (95%)
  local copies, waits for them, and re-layouts  2.27 us (5%)
    pallas_call x1, Pallas kernels, per_device(): pl.pallas_call(kernel, out_shape=jax.ShapeDtypeStruct((64, 8, 8, 128), jn...  45.8 us
    reshape x1, local copies, waits for them, and re-layouts, per_device(): return got.reshape(4096, 128).T[None]  2.27 us

profile of v6, /device:TPU:1, one launch (start us, length us, event | category | flops | bytes accessed | tf_op | source)
XLA Modules:
  0.0 48.1 jit_solution(3130901809655551832)
XLA Ops:
  0.0 45.8 %column_split.1 = bf16[64,8,8,128]{3,2,1,0:T(8,128)(2,1)} custom-call(bf16[28,4096]{1,0:T(8,128)(2,1)} %bitcast.8, bf16[7,4,4096]{2,1,0:T(4,128)(2,1)} %bitcast.9, s32[7,4,28]{2,1,0:T(4,128)} %bitcast.10, s32[4,7]{1,0:T(4,128)} %col_src.1), custom_call_target="tpu_custom_call" | custom-call | tf_op jit(solution)/shard_map/column_split/pallas_call | solution.py:309
  45.8 2.3 %copy.5 = bf16[4096,128]{0,1:T(8,128)(2,1)} copy(bf16[4096,128]{1,0:T(8,128)(2,1)} %bitcast.7) | data formatting | bytes 2097152 | tf_op jit(solution)/shard_map/reshape | solution.py:342

commit v7 on v6

--- a/solution.py
+++ b/solution.py
@@ -25,28 +25,38 @@
     return lax.rem(v + 4, 4)
 
 
-def columns_out(tiles):
-    lane = lax.broadcasted_iota(jnp.int32, tiles[0].shape, 1)
-    for i in range(5):
-        d, up = 2 << i, (lane & (2 << i)) != 0
-        swapped = list(tiles)
-        for t in range(32):
-            if not t & (1 << i):
-                low, high = tiles[t], tiles[t | (1 << i)]
-                swapped[t] = jnp.where(up, pltpu.roll(high, d, 1), low)
-                swapped[t | (1 << i)] = jnp.where(up, high, pltpu.roll(low, 128 - d, 1))
-        tiles = swapped
-    top, bottom = (lane & 64) != 0, (lane & 1) != 0
-    done = []
-    for v in tiles:
-        moved = jnp.where(top, pltpu.roll(v, 63, 1), pltpu.roll(v, 65, 1))
-        done.append(jnp.where(top == bottom, v, moved))
-    return done
+def bit_swap(n, pairs):
+    k = lax.broadcasted_iota(jnp.int32, (n, 128), 0)
+    to = k
+    for i, o in pairs:
+        odd = ((k >> i) ^ (k >> o)) & 1
+        to = to ^ (odd << i) ^ (odd << o)
+    lane = lax.broadcasted_iota(jnp.int32, (n, 128), 1)
+    parts = [jnp.where(to == lane + 128 * t, 1.0, 0.0).astype(jnp.bfloat16) for t in range(n // 128)]
+    return jnp.concatenate(parts, axis=1)
+
+
+def columns_out(tile, px):
+    tiles = [tile(t) for t in range(32)]
+    for high, pairs in ((3, ((8, 5), (7, 4))), (1, ((8, 3), (7, 2))), (0, ((7, 1), (6, 0)))):
+        step = 1 << high
+        count = 4 if high else 2
+        picks = [t for t in range(32) if not t & ((count - 1) * step)]
+        for i, t in enumerate(picks):
+            for n in range(count):
+                px[i * 32 : i * 32 + 32, n * 128 : n * 128 + 128] = tiles[t + n * step]
+        moved = jnp.dot(
+            px[0 : 32 * len(picks), 0 : 128 * count], bit_swap(128 * count, pairs), preferred_element_type=jnp.float32
+        )
+        for i, t in enumerate(picks):
+            for n in range(count):
+                tiles[t + n * step] = moved[i * 32 : i * 32 + 32, n * 128 : n * 128 + 128].astype(jnp.bfloat16)
+    return tiles
 
 
 def kernel(
     p_raw, a_raw, slot_raw, col_src, out,
-    praw, araw, sraw, craw, pf, pt, af, amine, imine,
+    praw, araw, sraw, craw, px, pf, pt, af, amine, imine,
     pall, abuf, ibuf, csm, wbuf, oh, prod_hi, prod_lo, of, obuf,
     ls, zs, zr, as_, ar, is_, ir, ss, rs, rl_, os, orr, smem_sem,
 ):
@@ -85,25 +95,16 @@
         pltpu.make_async_copy(ref, ref, sem).wait()
 
     loads[0].wait()
-    for m in (0, 8, 16, 24):
-        rows = min(8, 28 - m)
-        tiles = []
-        for t in range(32):
-            v = praw[m : m + rows, t * 128 : t * 128 + 128].astype(jnp.float32)
-            tiles.append(v if rows == 8 else jnp.concatenate([v, v], axis=0))
-        for t, v in enumerate(columns_out(tiles)):
-            at = (t % 4) * 28 + m
-            pf[t // 4, at : at + rows, :] = v[:rows]
+    def tile(t):
+        v = praw[:, t * 128 : t * 128 + 128].astype(jnp.float32)
+        return jnp.concatenate([v, jnp.zeros((4, 128), jnp.float32)], axis=0).astype(jnp.bfloat16)
+
+    for t, v in enumerate(columns_out(tile, px)):
+        pf[t // 4, t % 4 * 28 : t % 4 * 28 + 28, :] = v[:28].astype(jnp.float32)
     for t in range(8):
         pt[t] = pf[t].astype(jnp.bfloat16)
     pall[q, j] = pt[j]
     pl.semaphore_wait(barrier, 11)
-
-    remote(pt.at[partner], pall.at[q, j], zs, zr.at[0], in_column(partner)).start()
-    for e in (1, 3, 2):
-        for c in (0, 1):
-            t = 2 * m4(z - e) + c
-            remote(pt.at[t], pall.at[q, j], zs, zr.at[e], in_column(t)).start()
 
     def lead(e):
         return 0 if e in (0, 3) else 1
@@ -124,11 +125,17 @@
         send(e, rs.at[e, ident], aoff, 0, ALL, "b", 1)
         send(e, rs.at[e, ident + 1], aoff, 0, ALL, "b", -1)
 
+    def one_row_out(row):
+        ref = pall.at[q, row]
+        for axis, step, ident in ((0, 1, 0), (0, -1, 1), (1, 1, 4), (1, -1, 5)):
+            remote(ref, ref, ss, rs.at[0, ident], beside[(axis, step)]).start()
+
     def first(e):
         if e == 0:
             take(pall.at[q, partner], zr.at[0])
-        else:
-            take(pall.at[q, pl.ds(2 * chip[e], 2)], zr.at[e])
+            one_row_out(partner)
+            return
+        take(pall.at[q, pl.ds(2 * chip[e], 2)], zr.at[e])
         send(e, rs.at[e, 0], 0, 0, ALL, "a", 1)
         send(e, rs.at[e, 1], 0, 0, ALL, "a", -1)
         both(e, 4, 0)
@@ -151,6 +158,13 @@
         send(e, rl_, aoff, -1, LO, "b", 1)
         take(spot(e, aoff, 1, ALL), rs.at[e, 5 + 2 * i])
         send(e, rl_, aoff, 1, HI, "b", -1)
+
+    remote(pt.at[partner], pall.at[q, j], zs, zr.at[0], in_column(partner)).start()
+    one_row_out(j)
+    for e in (1, 3, 2):
+        for c in (0, 1):
+            t = 2 * m4(z - e) + c
+            remote(pt.at[t], pall.at[q, j], zs, zr.at[e], in_column(t)).start()
 
     first(0)
 
@@ -316,6 +330,7 @@
             pltpu.VMEM((7, 4, 4096), jnp.bfloat16),
             pltpu.VMEM((7, 4, 28), jnp.int32),
             pltpu.VMEM((4, 7), jnp.int32),
+            pltpu.VMEM((512, 512), jnp.bfloat16),
             pltpu.VMEM((8, ROWS, 128), jnp.float32),
             pltpu.VMEM((8, ROWS, 128), jnp.bfloat16),
             pltpu.VMEM((7, 128, 128), jnp.float32),

time: 48.2 us -> 48.3 us (level)
  no operation moved by 1% of the time
where the time goes in v7:
time: 48.3 us; the launch traced here: 48.2 us
  Pallas kernels  45.9 us (95%)
  local copies, waits for them, and re-layouts  2.27 us (5%)
    pallas_call x1, Pallas kernels, per_device(): pl.pallas_call(kernel, out_shape=jax.ShapeDtypeStruct((64, 8, 8, 128), jn...  45.9 us
    reshape x1, local copies, waits for them, and re-layouts, per_device(): return got.reshape(4096, 128).T[None]  2.27 us

profile of v7, /device:TPU:1, one launch (start us, length us, event | category | flops | bytes accessed | tf_op | source)
XLA Modules:
  0.0 48.2 jit_solution(10575863405436410612)
XLA Ops:
  0.0 45.9 %column_split.1 = bf16[64,8,8,128]{3,2,1,0:T(8,128)(2,1)} custom-call(bf16[28,4096]{1,0:T(8,128)(2,1)} %bitcast.8, bf16[7,4,4096]{2,1,0:T(4,128)(2,1)} %bitcast.9, s32[7,4,28]{2,1,0:T(4,128)} %bitcast.10, s32[4,7]{1,0:T(4,128)} %col_src.1), custom_call_target="tpu_custom_call" | custom-call | tf_op jit(solution)/shard_map/column_split/pallas_call | solution.py:323
  45.9 2.3 %copy.5 = bf16[4096,128]{0,1:T(8,128)(2,1)} copy(bf16[4096,128]{1,0:T(8,128)(2,1)} %bitcast.7) | data formatting | bytes 2097152 | tf_op jit(solution)/shard_map/reshape | solution.py:357
